TPU v7x, 128 devices: a whole 4x4x4 slice. The times are simulated.
128 devices in a mesh: rep: 8 (over x, y_lo), shard: 16 (over y_hi, z, core).
Axes of the slice: x: 4, y: 4 (y_hi: 2, y_lo: 2; y = y_hi * 2 + y_lo), z: 4, core: 2. Of those that a mesh axis runs over, the one named last changes fastest.
Arguments:
- tokens: bfloat16 [2, 8192, 1536], P(None, ('rep', 'shard')), may hold values from -6 to 6
- query_weight: bfloat16 [1536, 1536], P('shard'), may hold values from -0.15625 to 0.15625
- key_weight: bfloat16 [1536, 768], P('shard'), may hold values from -0.15625 to 0.15625
- value_weight: bfloat16 [1536, 768], P('shard'), may hold values from -0.15625 to 0.15625
- out_weight: bfloat16 [1536, 1536], P('shard'), may hold values from -0.4375 to 0.4375
- gate_weight: bfloat16 [1536, 4096], P('shard'), may hold values from -0.15625 to 0.15625
- up_weight: bfloat16 [1536, 4096], P('shard'), may hold values from -0.15625 to 0.15625
- down_weight: bfloat16 [4096, 1536], P('shard'), may hold values from -0.09375 to 0.09375
- attention_gain: bfloat16 [1536], P('shard'), may hold values from 0.5 to 1.5
- feedforward_gain: bfloat16 [1536], P('shard'), may hold values from 0.5 to 1.5
- lengths: int32 [2, 8, 32], P(None, 'rep'), may hold values from 19 to 43, as said below
- deal: int32 [2, 8, 32], P(None, 'rep'), may hold values from 0 to 31, as said below
- block_cotangent: bfloat16 [2, 8192, 1536], P(None, ('rep', 'shard')), may hold values from -6 to 6
Outputs:
- block_out: bfloat16 [2, 8192, 1536], P(None, ('rep', 'shard'))
- input_grad: bfloat16 [2, 8192, 1536], P(None, ('rep', 'shard'))
- grad_query: float32 [1536, 1536], P('shard')
- grad_key: float32 [1536, 768], P('shard')
- grad_value: float32 [1536, 768], P('shard')
- grad_output: float32 [1536, 1536], P('shard')
- grad_gate: float32 [1536, 4096], P('shard')
- grad_up: float32 [1536, 4096], P('shard')
- grad_down: float32 [4096, 1536], P('shard')
- grad_attention_gain: float32 [1536], P('shard')
- grad_feedforward_gain: float32 [1536], P('shard')
Inputs may be any that keep to these rules, and one draw needn't show every extreme that they name: `lengths`: for each micro-batch and replica group, the 2 sequences that deal places into one bin have between (585) // 10 and 64 tokens together, and some bin of the group has exactly 64. `deal`: for each micro-batch and replica group, a permutation of the group's 32 sequence numbers; entry b * 2 + s names the sequence in place s of bin b.
All inputs are finite; a program needn't handle non-finite values.
Results may differ from a plain program's by a relative error of at most 0.023.
Values may be sent and summed in bfloat16 or wider, within the bound.
A program may use at most 320 MiB of HBM per device.

v0:
```python
import math

import jax
import jax.numpy as jnp
from jax import lax
from jax.experimental import pallas as pl
from jax.experimental.pallas import tpu as pltpu
from jax.sharding import PartitionSpec as P

D = 1536
QUERY_HEADS = 16
KEY_VALUE_HEADS = 8
HEAD_WIDTH = 96
QW = QUERY_HEADS * HEAD_WIDTH
KVW = KEY_VALUE_HEADS * HEAD_WIDTH
FF = 4096
BIN = 64
HALO = 48
WIN = BIN + HALO
MB = 2
SHARDS = 16
ROWS = MB * WIN
MESH = pl.DeviceIdType.MESH
ANY = pl.BlockSpec(memory_space=pl.ANY)
DMA = pltpu.SemaphoreType.DMA

eps_norm = 1e-05
rope_base = 100000.0


class Place:
    def __init__(self):
        rep, shard = lax.axis_index("rep"), lax.axis_index("shard")
        self.rep, self.shard = rep, shard
        self.x, self.yl = rep // 2, rep % 2
        self.yh, self.z, self.c = shard // 8, (shard // 2) % 4, shard % 2
        self.y = self.yh * 2 + self.yl
        self.half = jnp.where(self.yh == self.yl, 1, 0)

    def at(self, x=None, yh=None, yl=None, z=None, c=None):
        def pick(new, old):
            return old if new is None else new

        rep = pick(x, self.x) * 2 + pick(yl, self.yl)
        return rep, pick(yh, self.yh) * 8 + pick(z, self.z) * 2 + pick(c, self.c)

    def along(self, dim):
        found = []
        for o in (1, 2, 3):
            x, yh, yl, z = self.x, self.yh, self.yl, self.z
            if dim == "x":
                x = (x + o) % 4
            elif dim == "z":
                z = (z + o) % 4
            else:
                y = (self.y + o) % 4
                yh, yl = y // 2, y % 2
            found.append((x, yh, yl, z))
        return found

    def peers(self, dim):
        return [self.at(*where) for where in self.along(dim)]

    def cross(self):
        return self.at(yh=1 - self.yh, yl=1 - self.yl)

    def inner(self):
        return self.at(yl=1 - self.yl)

    def sibling(self):
        return self.at(c=1 - self.c)

    def step(self, by):
        return self.rep, (self.shard + by + SHARDS) % SHARDS


def meet(peers):
    barrier = pltpu.get_barrier_semaphore()
    for peer in peers:
        pl.semaphore_signal(barrier, inc=1, device_id=peer, device_id_type=MESH)
    pl.semaphore_wait(barrier, len(peers))


class Sender:
    def __init__(self):
        self.pending = []

    def __call__(self, src, dst, send_sem, recv_sem, to):
        copy = pltpu.make_async_remote_copy(
            src_ref=src,
            dst_ref=dst,
            send_sem=send_sem,
            recv_sem=recv_sem,
            device_id=to,
            device_id_type=MESH,
        )
        copy.start()
        self.pending.append(copy)
        return copy

    def drain(self):
        for copy in self.pending:
            copy.wait_send()


def cut(first, count):
    if isinstance(first, int):
        return pl.ds(first, count)
    return pl.ds(pl.multiple_of(first, 128), count)


def rcut(first, count):
    if isinstance(first, int):
        return pl.ds(first, count)
    return pl.ds(pl.multiple_of(first, 16), count)


def exchange_kernel(whole, *refs):
    count = len(whole)
    ins, outs = refs[:count], refs[count : 2 * count]
    send_sem, recv_sem, local_sem = refs[2 * count : 2 * count + 3]
    staged = refs[2 * count + 3 :]
    me = Place()
    local = []
    for i, (src, dst) in enumerate(zip(ins, outs)):
        width = dst.shape[-1]
        own = src if whole[i] else src.at[:, cut(me.c * width, width)]
        local.append(pltpu.make_async_copy(own, staged[i], local_sem.at[i, 0]))
        local[i].start()
    meet([me.sibling()])
    send = Sender()
    for i, (src, dst) in enumerate(zip(ins, outs)):
        width = dst.shape[-1]
        theirs = src if whole[i] else src.at[:, cut((1 - me.c) * width, width)]
        send(theirs, dst.at[me.c], send_sem.at[i], recv_sem.at[i], me.sibling())
    for i, dst in enumerate(outs):
        local[i].wait()
        local[i] = pltpu.make_async_copy(staged[i], dst.at[me.c], local_sem.at[i, 1])
        local[i].start()
    for i, copy in enumerate(send.pending):
        local[i].wait()
        copy.wait_recv()
    send.drain()


def exchange(arrays, whole):
    count = len(arrays)
    outs = []
    for array, full in zip(arrays, whole):
        rows, width = array.shape
        outs.append(jax.ShapeDtypeStruct((2, rows, width if full else width // 2), array.dtype))
    results = pl.pallas_call(
        lambda *refs: exchange_kernel(whole, *refs),
        out_shape=outs,
        in_specs=[ANY] * count,
        out_specs=[ANY] * count,
        scratch_shapes=[DMA((count,))] * 2 + [DMA((count, 2))] + [pltpu.VMEM(out.shape[1:], out.dtype) for out in outs],
        compiler_params=pltpu.CompilerParams(collective_id=2, has_side_effects=True, vmem_limit_bytes=24 * 2**20),
        name="exchange_rows",
    )(*arrays)
    return [both.reshape(-1, both.shape[-1]) for both in results]


REDUCE_ROWS = (192, 192, 192, 192, 192, 512, 64)
REDUCE_COLUMNS = (768, 768, 768, 2048, 2048, 768, 256)
REDUCE_DIMS = {"A": "zyx", "B": "yxz", "C": "xzy"}
REDUCE_UNITS = [("A", 3, i * 512, 512) for i in range(4)] + [("A", 0, 0, 768)]
REDUCE_UNITS += [("B", 4, i * 512, 512) for i in range(4)] + [("B", 1, 0, 768)]
REDUCE_UNITS += [("C", 5, i * 256, 256) for i in range(3)] + [("C", 2, 0, 768), ("C", 6, 0, 256)]
ROUNDS = [(t, 5 + t, 10 + t) for t in range(5)]
GAINS = 6


def reduce_shapes(u):
    order, a, _, n = REDUCE_UNITS[u]
    r = REDUCE_ROWS[a]
    first = {"A": (2, r, n), "B": (4, r, n // 2), "C": (2, 4, r // 4, n)}[order]
    second = {"A": (r, n // 2), "B": (4, r // 4, n // 2), "C": (2, r // 4, n)}[order]
    return first, second, (r // 4, n // 2)


def add_into(total, parts):
    *lead, rows, _ = total.shape
    blocks = rows // 16

    def step(i, carry):
        where, rest = [], i // blocks
        for n in reversed(lead):
            where.insert(0, rest % n)
            rest = rest // n
        where = (*where, rcut((i % blocks) * 16, 16), slice(None))
        s = total[where].astype(jnp.float32)
        for k in range(3):
            s = s + parts[(k, *where)].astype(jnp.float32)
        total[where] = s.astype(jnp.bfloat16)
        return carry

    lax.fori_loop(0, math.prod(lead) * blocks, step, 0)


def reduce_kernel(*refs):
    nu = len(REDUCE_UNITS)
    ins, rows_in, outs, halo, totals = refs[:7], refs[7:9], refs[9:16], refs[16], refs[17:24]
    rest = refs[24:]
    kept = (rest[:nu], rest[nu : 2 * nu], rest[2 * nu : 3 * nu])
    taken = (rest[3 * nu : 4 * nu], rest[4 * nu : 5 * nu], rest[5 * nu : 6 * nu])
    send_sem, recv_sem, g_send, g_recv, s_send, s_recv, h_send, h_recv, local_sem, final_sem = rest[6 * nu :]
    me = Place()
    meet(me.peers("z") + me.peers("x") + me.peers("y") + [me.sibling(), me.step(-1), me.step(1)])
    send = Sender()
    sent, own = {}, {}

    def share(u, stage, x, yh, yl, z):
        order, a, first, n = REDUCE_UNITS[u]
        r = REDUCE_ROWS[a] // 4
        src = ins[a] if stage == 0 else kept[stage - 1][u]
        begin = first if stage == 0 else 0
        dim = REDUCE_DIMS[order][stage]
        lead = {"A": 2, "B": 2, "C": 2}[order] if stage == 0 else len(src.shape) - 2
        columns = slice(None) if stage else cut(begin, n)
        if dim == "z":
            return src.at[:, z, :, columns] if lead == 2 else src.at[z]
        if dim == "x":
            rows = rcut(x * r, r)
            if lead == 2:
                return src.at[:, :, rows, columns]
            return src.at[:, rows] if lead == 1 else src.at[rows]
        columns = cut(begin + yl * (n // 2), n // 2)
        if lead == 2:
            return src.at[yh, :, :, columns]
        return src.at[yh, :, columns]

    def issue(u, stage):
        dim = REDUCE_DIMS[REDUCE_UNITS[u][0]][stage]
        sent[u, stage] = [
            send(share(u, stage, *where), taken[stage][u].at[i], send_sem.at[u, stage, i], recv_sem.at[u, stage, i], me.at(*where))
            for i, where in enumerate(me.along(dim))
        ]
        own[u, stage] = pltpu.make_async_copy(
            share(u, stage, me.x, me.yh, me.yl, me.z), kept[stage][u], local_sem.at[u, stage]
        )
        own[u, stage].start()

    def finish(u, stage):
        own[u, stage].wait()
        for copy in sent[u, stage]:
            copy.wait_recv()
        add_into(kept[stage][u], taken[stage][u])

    def result(u, all_x, all_y):
        order, a, first, n = REDUCE_UNITS[u]
        r = REDUCE_ROWS[a] // 4
        rows = slice(None) if all_x else rcut(me.x * r, r)
        columns = cut(first, n) if all_y else cut(first + me.yl * (n // 2), n // 2)
        return totals[a].at[rows, columns]

    def spread_one(u):
        order = REDUCE_UNITS[u][0]
        dst = result(u, False, False)
        own[u, 3] = pltpu.make_async_copy(kept[2][u], dst, local_sem.at[u, 3])
        own[u, 3].start()
        to = [me.inner()] if order == "C" else me.peers("x")
        sent[u, 3] = [send(kept[2][u], dst, g_send.at[u, i], g_recv.at[u, i], one) for i, one in enumerate(to)]

    def spread_two(u):
        order = REDUCE_UNITS[u][0]
        own[u, 3].wait()
        for copy in sent[u, 3]:
            copy.wait_recv()
        ref = result(u, order != "C", order == "C")
        to = me.peers("x") if order == "C" else [me.inner()]
        sent[u, 4] = [send(ref, ref, g_send.at[u, 3 + i], g_recv.at[u, 3 + i], one) for i, one in enumerate(to)]

    last = []

    def deliver(u):
        order, a, first, n = REDUCE_UNITS[u]
        for copy in sent[u, 4]:
            copy.wait_recv()
        if a == GAINS:
            own[u, 5] = pltpu.make_async_copy(totals[a], outs[a], final_sem.at[u])
            own[u, 5].start()
            return
        r, width = REDUCE_ROWS[a] // 2, REDUCE_COLUMNS[a]
        dst = outs[a].at[:, cut(me.c * width + first, n)]
        last.append(send(totals[a].at[rcut((1 - me.c) * r, r), cut(first, n)], dst, s_send.at[u], s_recv.at[u], me.sibling()))
        own[u, 5] = pltpu.make_async_copy(totals[a].at[rcut(me.c * r, r), cut(first, n)], dst, final_sem.at[u])
        own[u, 5].start()

    for i, src in enumerate(rows_in):
        last.append(send(src.at[:, pl.ds(BIN, HALO)], halo.at[i], h_send.at[i], h_recv.at[i], me.step(1)))
    count = len(ROUNDS)
    for u in ROUNDS[0]:
        issue(u, 0)
    for t in range(count + 4):
        if t + 1 < count:
            for u in ROUNDS[t + 1]:
                issue(u, 0)
        for stage in range(2):
            if 0 <= t - stage < count:
                for u in ROUNDS[t - stage]:
                    finish(u, stage)
                    issue(u, stage + 1)
        if 0 <= t - 2 < count:
            for u in ROUNDS[t - 2]:
                finish(u, 2)
                spread_one(u)
        if 0 <= t - 3 < count:
            for u in ROUNDS[t - 3]:
                spread_two(u)
        if 0 <= t - 4 < count:
            for u in ROUNDS[t - 4]:
                deliver(u)
    for u in range(nu):
        own[u, 5].wait()
    for copy in last:
        copy.wait_recv()
    send.drain()


def reduce_grads(grads, block_rows, input_rows):
    nu = len(REDUCE_UNITS)
    first, second, third = zip(*[reduce_shapes(u) for u in range(nu)])
    low = jnp.bfloat16
    shapes = list(zip(REDUCE_ROWS, REDUCE_COLUMNS))
    outs = [jax.ShapeDtypeStruct((r // 2, 2 * n), low) for r, n in shapes[:GAINS]]
    outs.append(jax.ShapeDtypeStruct(shapes[GAINS], low))
    outs.append(jax.ShapeDtypeStruct((2, MB, HALO, D), low))
    scratch = [pltpu.VMEM(s, low) for s in shapes]
    scratch += [pltpu.VMEM(s, low) for s in (*first, *second, *third)]
    scratch += [pltpu.VMEM((3, *s), low) for s in (*first, *second, *third)]
    scratch += [DMA((nu, 3, 3))] * 2 + [DMA((nu, 6))] * 2 + [DMA((nu,))] * 2 + [DMA((2,))] * 2 + [DMA((nu, 4)), DMA((nu,))]
    results = pl.pallas_call(
        reduce_kernel,
        out_shape=outs,
        in_specs=[ANY] * 9,
        out_specs=[ANY] * len(outs),
        scratch_shapes=scratch,
        compiler_params=pltpu.CompilerParams(collective_id=3, has_side_effects=True, vmem_limit_bytes=56 * 2**20),
        name="reduce_grads",
    )(*grads, block_rows, input_rows)
    return results[:GAINS], results[GAINS], results[GAINS + 1]


def window_layout(seq_lengths, first_row):
    count = seq_lengths.shape[0]
    ids = jnp.arange(count, dtype=jnp.int32)
    earlier = ids[None, :] < ids[:, None]
    start = jnp.sum(jnp.where(earlier, seq_lengths[None, :], 0), axis=1)
    end = start + seq_lengths
    rows = first_row + jnp.arange(WIN, dtype=jnp.int32)
    which = jnp.sum((rows[:, None] >= end[None, :]).astype(jnp.int32), axis=1)
    onehot = which[:, None] == ids[None, :]
    begin = jnp.sum(jnp.where(onehot, start[None, :], 0), axis=1)
    inside = which < count
    mine = inside & (begin >= first_row) & (begin < first_row + BIN)
    return which, rows - begin, mine, inside


def dot(a, b, dims):
    return lax.dot_general(a, b, (dims, ((), ())), preferred_element_type=jnp.float32)


def nn(a, b):
    return dot(a, b, ((1,), (0,)))


def nt(a, b):
    return dot(a, b, ((1,), (1,)))


def tn(a, b):
    return dot(a, b, ((0,), (0,)))


FF_BLOCK = 512
FF_BLOCKS = FF // FF_BLOCK
CHUNK = 4 * HEAD_WIDTH
SCALE = HEAD_WIDTH ** (-0.5)


def mean_of(value):
    return jnp.mean(value, axis=-1, keepdims=True)


def swap_halves(value):
    lane = lax.broadcasted_iota(jnp.int32, value.shape, 1) % HEAD_WIDTH
    return jnp.where(
        lane < HEAD_WIDTH // 2, pltpu.roll(value, CHUNK - HEAD_WIDTH // 2, 1), pltpu.roll(value, HEAD_WIDTH // 2, 1)
    )


def split_heads(dst, chunk, value):
    for i in range(4):
        dst[4 * chunk + i, :, :HEAD_WIDTH] = value[:, HEAD_WIDTH * i : HEAD_WIDTH * (i + 1)].astype(jnp.bfloat16)


def allowed_pairs(seg_ref, segt_ref):
    row = lax.broadcasted_iota(jnp.int32, (ROWS, ROWS), 0)
    column = lax.broadcasted_iota(jnp.int32, (ROWS, ROWS), 1)
    return (seg_ref[...] == segt_ref[...]) & (column <= row)


def probabilities(q, k, allowed):
    s = jnp.where(allowed, nt(q, k) * SCALE, -1e30)
    e = jnp.exp(s - jnp.max(s, axis=-1, keepdims=True))
    return e / jnp.sum(e, axis=-1, keepdims=True)


def second_norm(x2_ref, gain_ref, a2_ref):
    x2 = x2_ref[...]
    r2 = lax.rsqrt(mean_of(x2 * x2) + eps_norm)
    a2_ref[...] = (x2 * r2 * gain_ref[...]).astype(jnp.bfloat16)


def feedforward_block(first, a2_ref, dy_ref, wg, wu, wd, hid_ref, dg_ref, du_ref, yb_ref, da2_ref):
    at = cut(first, FF_BLOCK)
    g = nn(a2_ref[...], wg)
    u = nn(a2_ref[...], wu)
    sig = jax.nn.sigmoid(g)
    sw = g * sig
    hid = (sw * u).astype(jnp.bfloat16)
    hid_ref[:, at] = hid
    dhid = nt(dy_ref[...], wd)
    dg = (dhid * u * sig * (1.0 + g * (1.0 - sig))).astype(jnp.bfloat16)
    du = (dhid * sw).astype(jnp.bfloat16)
    dg_ref[:, at] = dg
    du_ref[:, at] = du
    yb_ref[...] += nn(hid, wd)
    da2_ref[...] += nt(dg, wg) + nt(du, wu)


def feedforward_back(dy_ref, x2_ref, da2_ref, gain_ref, dat_ref, dgain_ref):
    x2, da2 = x2_ref[...], da2_ref[...]
    r2 = lax.rsqrt(mean_of(x2 * x2) + eps_norm)
    n2 = x2 * r2
    dgain_ref[1:2, :] = jnp.sum(da2 * n2, axis=0, keepdims=True)
    e2 = da2 * gain_ref[...]
    dx2 = dy_ref[...].astype(jnp.float32) + r2 * (e2 - n2 * mean_of(e2 * n2))
    da2_ref[...] = dx2
    dat_ref[...] = dx2.astype(jnp.bfloat16)


def attention_backward(
    x_ref, gain_ref, cos_ref, sin_ref, seg_ref, segt_ref, wq, wk, wv, wo, q_ref, k_ref, v_ref, dat_ref, dx2_ref, do_ref, turn_ref, dqf_ref, dkv_ref, dx_ref, dgain_ref
):
    for chunk in range(4):
        rows = wo[chunk // 2, 2 * (chunk % 2) : 2 * (chunk % 2) + 2].reshape(CHUNK, D)
        split_heads(do_ref, chunk, nt(dat_ref[...], rows))
    allowed = allowed_pairs(seg_ref, segt_ref)
    for c in range(KEY_VALUE_HEADS):
        k, v = k_ref[c], v_ref[c]
        dk = jnp.zeros((ROWS, 128), jnp.float32)
        dv = jnp.zeros((ROWS, 128), jnp.float32)
        for head in (2 * c, 2 * c + 1):
            q, do = q_ref[head], do_ref[head]
            p = probabilities(q, k, allowed)
            dp = nt(do, v)
            ds = (p * (dp - jnp.sum(p * dp, axis=-1, keepdims=True))).astype(jnp.bfloat16)
            dq = nn(ds, k) * SCALE
            turn_ref[:, HEAD_WIDTH * head : HEAD_WIDTH * (head + 1)] = dq[:, :HEAD_WIDTH]
            dk = dk + tn(ds, q)
            dv = dv + tn(p.astype(jnp.bfloat16), do)
        dkv_ref[:, KVW + HEAD_WIDTH * c : KVW + HEAD_WIDTH * (c + 1)] = dv[:, :HEAD_WIDTH].astype(jnp.bfloat16)
        turn_ref[:, QW + HEAD_WIDTH * c : QW + HEAD_WIDTH * (c + 1)] = (dk * SCALE)[:, :HEAD_WIDTH]
    cos, sin = cos_ref[...], sin_ref[...]
    for chunk in range(6):
        value = turn_ref[:, CHUNK * chunk : CHUNK * (chunk + 1)]
        value = (value * cos - swap_halves(value) * sin).astype(jnp.bfloat16)
        if chunk < 4:
            dqf_ref[:, CHUNK * chunk : CHUNK * (chunk + 1)] = value
        else:
            dkv_ref[:, CHUNK * (chunk - 4) : CHUNK * (chunk - 3)] = value
    da1 = nt(dqf_ref[...], wq[...].reshape(D, QW)) + nt(dkv_ref[:, :KVW], wk[...].reshape(D, KVW))
    da1 = da1 + nt(dkv_ref[:, KVW:], wv[...].reshape(D, KVW))
    x = x_ref[...].astype(jnp.float32)
    r1 = lax.rsqrt(mean_of(x * x) + eps_norm)
    n1 = x * r1
    dgain_ref[0:1, :] = jnp.sum(da1 * n1, axis=0, keepdims=True)
    e1 = da1 * gain_ref[...]
    dx = dx2_ref[...] + r1 * (e1 - n1 * mean_of(e1 * n1))
    dx_ref[...] = dx.astype(jnp.bfloat16)


GATHER_UNITS = [(7, 0, 256, False), (1, 0, 768, False), (2, 0, 768, False), (4, 0, 512, True), (0, 0, 768, False), (0, 768, 768, False)]
GATHER_UNITS += [(4, 2048, 512, True), (3, 0, 768, False), (3, 768, 768, False), (5, 0, 512, True)]
GATHER_UNITS += [(6, i * 256, 256, False) for i in range(6)] + [(5, 2048 + i * 512, 512, False) for i in range(4)]
AHEAD = 3
GATE_ONE, GATE_TWO, UP_X, DOWN_LAST, UP_LAST = 3, 6, 9, 15, 19


def layer_kernel(*refs):
    parts, (tokens, cotangent, cos_ref, sin_ref, seg_ref, segt_ref, mine_ref) = refs[:8], refs[8:15]
    wg_hbm, wu_hbm, wd_hbm = refs[15:18]
    block_ref, dx_ref, a1_ref, o_ref, a2_ref, hid_ref, dqf_ref, dkv_ref, dat_ref, dg_ref, du_ref, dgain_ref, dy_ref = refs[18:31]
    wq, wk, wv, wo, gains_ref, x_ref, gain1_ref, gain2_ref, wg, wu, wd, q_ref, k_ref, v_ref, do_ref, x2_ref, da2_ref, turn_ref = refs[31:49]
    z_send, z_recv, y_send, y_recv, s_send, s_recv, x_send, x_recv, h_send, h_recv, local_sem, row_sem, block_sem = refs[49:62]
    staged = refs[62:]
    outs = (wq, wk, wv, wo, wg_hbm, wu_hbm, wd_hbm, gains_ref)
    me = Place()
    units = GATHER_UNITS
    count = len(units)
    local, z_sent, y_one, y_two, x_sent, s_sent = {}, {}, {}, {}, {}, {}

    def columns(u, half=None, quarter=None):
        array, first, width, over_x = units[u]
        if over_x:
            first = first + (me.x if quarter is None else quarter) * width
        if half is None:
            return cut(first, width)
        return cut(first + half * (width // 2), width // 2)

    for u in range(count):
        local[u] = pltpu.make_async_copy(parts[units[u][0]].at[:, columns(u)], staged[u], local_sem.at[u, 0])
        local[u].start()
    rows = []
    for i, (src, dst) in enumerate(((tokens, x_ref), (cotangent, dy_ref))):
        for m in range(MB):
            rows.append(pltpu.make_async_copy(src.at[m], dst.at[pl.ds(m * WIN, BIN)], row_sem.at[i, m]))
            rows[-1].start()
    meet(me.peers("z") + me.peers("x") + [me.cross(), me.inner(), me.sibling(), me.step(-1), me.step(1)])
    send = Sender()

    def to_sibling(u, at, ref):
        s_sent[u, at] = send(ref, ref, s_send.at[u, at], s_recv.at[u, at], me.sibling())

    def z_phase(u):
        a = units[u][0]
        dst = outs[a].at[me.yh, me.z, me.c, :, columns(u)]
        local[u].wait()
        z_sent[u] = [send(staged[u], dst, z_send.at[u, i], z_recv.at[u, i], to) for i, to in enumerate(me.peers("z"))]
        local[u] = pltpu.make_async_copy(staged[u], dst, local_sem.at[u, 1])
        local[u].start()

    def y_phase(u):
        a = units[u][0]
        local[u].wait()
        for copy in z_sent[u]:
            copy.wait_recv()
        ref = outs[a].at[me.yh, :, me.c, :, columns(u, me.half)]
        y_one[u] = send(ref, ref, y_send.at[u, 0], y_recv.at[u, 0], me.cross())
        if not units[u][3]:
            to_sibling(u, 0, outs[a].at[me.yh, :, me.c, :, columns(u)])

    def forward_phase(u):
        a = units[u][0]
        y_one[u].wait_recv()
        ref = outs[a].at[1 - me.yh, :, me.c, :, columns(u, me.half)]
        y_two[u] = send(ref, ref, y_send.at[u, 1], y_recv.at[u, 1], me.inner())

    def last_phase(u):
        a = units[u][0]
        y_two[u].wait_recv()
        if units[u][3]:
            ref = outs[a].at[:, :, me.c, :, columns(u)]
            x_sent[u] = [send(ref, ref, x_send.at[u, i], x_recv.at[u, i], to) for i, to in enumerate(me.peers("x"))]
            to_sibling(u, 3, ref)
        else:
            to_sibling(u, 1, outs[a].at[1 - me.yh, :, me.c, :, columns(u)])

    def x_phase(u, i):
        x_sent[u][i].wait_recv()
        to_sibling(u, i, outs[units[u][0]].at[:, :, me.c, :, columns(u, None, (me.x + 3 - i) % 4)])

    def arrived(*which):
        for u in which:
            for at in range(4):
                if (u, at) in s_sent:
                    s_sent.pop((u, at)).wait_recv()

    cos, sin = cos_ref[...], sin_ref[...]

    def begin():
        for copy in rows:
            copy.wait()
        for copy in halo:
            copy.wait_recv()
        keep = mine_ref[...] > 0
        x_ref[...] = jnp.where(keep, x_ref[...], jnp.zeros_like(x_ref))
        dy_ref[...] = jnp.where(keep, dy_ref[...], jnp.zeros_like(dy_ref))
        arrived(0)
        for s in range(SHARDS):
            row = gains_ref[s // 8, (s // 2) % 4, s % 2, 0:1, :].astype(jnp.float32)
            gain1_ref[:, 96 * s : 96 * (s + 1)] = row[:, :96]
            gain2_ref[:, 96 * s : 96 * (s + 1)] = row[:, 128:224]
        x = x_ref[...].astype(jnp.float32)
        a1_ref[...] = (x * lax.rsqrt(mean_of(x * x) + eps_norm) * gain1_ref[...]).astype(jnp.bfloat16)
        for ref in (q_ref, k_ref, v_ref, do_ref):
            ref[:, :, HEAD_WIDTH:] = jnp.zeros((ref.shape[0], ROWS, 128 - HEAD_WIDTH), jnp.bfloat16)

    def project(weight, dst, chunk, turned):
        value = nn(a1_ref[...], weight[:, :, :, :, CHUNK * chunk : CHUNK * (chunk + 1)].reshape(D, CHUNK))
        if turned:
            value = value * cos + swap_halves(value) * sin
        split_heads(dst, chunk, value)

    def attend(first):
        allowed = allowed_pairs(seg_ref, segt_ref)
        for head in range(first, first + 4):
            p = probabilities(q_ref[head], k_ref[head // 2], allowed)
            o = nn(p.astype(jnp.bfloat16), v_ref[head // 2])
            o_ref[:, HEAD_WIDTH * head : HEAD_WIDTH * (head + 1)] = o[:, :HEAD_WIDTH].astype(jnp.bfloat16)

    def out_project(part):
        at = slice(768 * part, 768 * (part + 1))
        x2_ref[:, at] = x_ref[:, at].astype(jnp.float32) + nn(o_ref[...], wo[:, :, :, :, at].reshape(QW, 768))

    yb_ref = turn_ref.at[:, :D]

    def between():
        second_norm(x2_ref, gain2_ref, a2_ref)
        yb_ref[...] = x2_ref[...]
        da2_ref[...] = jnp.zeros_like(da2_ref)

    loads = []

    def block_load(first):
        slot = len(loads) % 2
        pair = first // FF_BLOCK
        copies = [
            pltpu.make_async_copy(wg_hbm.at[:, :, :, :, cut(first, FF_BLOCK)], wg.at[slot], block_sem.at[slot, 0]),
            pltpu.make_async_copy(wu_hbm.at[:, :, :, :, cut(first, FF_BLOCK)], wu.at[slot], block_sem.at[slot, 1]),
            pltpu.make_async_copy(wd_hbm.at[pair // 4, pair % 4], wd.at[slot], block_sem.at[slot, 2]),
        ]
        for copy in copies:
            copy.start()
        loads.append((first, slot, copies))

    done = []

    def block_compute():
        first, slot, copies = loads[len(done)]
        done.append(first)
        for copy in copies:
            copy.wait()
        feedforward_block(
            first, a2_ref, dy_ref, wg[slot].reshape(D, FF_BLOCK), wu[slot].reshape(D, FF_BLOCK), wd[slot].reshape(FF_BLOCK, D),
            hid_ref, dg_ref, du_ref, yb_ref, da2_ref,
        )

    halo = []
    for i, (src, dst) in enumerate(((tokens, x_ref), (cotangent, dy_ref))):
        for m in range(MB):
            there = dst.at[pl.ds(m * WIN + BIN, HALO)]
            halo.append(send(src.at[m, pl.ds(0, HALO)], there, h_send.at[i, m], h_recv.at[i, m], me.step(-1)))

    def quarter(i):
        return ((me.x + 3 - i) % 4) * FF_BLOCK

    def x_quarters(u):
        for i in range(3):
            x_phase(u, i)

    pieces = {
        3: [begin],
        4: [lambda: arrived(1), lambda: project(wk, k_ref, 0, True), lambda: project(wk, k_ref, 1, True)],
        5: [lambda: arrived(2), lambda: project(wv, v_ref, 0, False), lambda: project(wv, v_ref, 1, False)],
        7: [lambda: arrived(4), lambda: project(wq, q_ref, 0, True)],
        8: [lambda: project(wq, q_ref, 1, True), lambda: arrived(5)],
        9: [lambda: project(wq, q_ref, 2, True)],
        10: [lambda: project(wq, q_ref, 3, True)],
        11: [lambda: attend(0), lambda: x_quarters(GATE_ONE)],
        12: [lambda: attend(4)],
        13: [lambda: attend(8)],
        14: [lambda: attend(12)],
        15: [lambda: x_quarters(GATE_TWO), lambda: arrived(7, 8), lambda: out_project(0)],
        16: [lambda: out_project(1)],
        17: [between],
        18: [lambda: arrived(GATE_ONE, UP_X, *range(10, 16)), lambda: block_load(me.x * FF_BLOCK)],
        19: [lambda: arrived(GATE_TWO, 16), lambda: block_load(2048), block_compute],
        20: [lambda: arrived(17), lambda: x_quarters(UP_X), lambda: block_load(2048 + FF_BLOCK) , block_compute],
        21: [block_compute, lambda: arrived(18), lambda: block_load(2048 + 2 * FF_BLOCK)],
    }
    for u in range(AHEAD):
        z_phase(u)
    for t in range(count + 2):
        if t + AHEAD < count:
            z_phase(t + AHEAD)
        if t < count:
            y_phase(t)
        if 1 <= t <= count:
            forward_phase(t - 1)
        if t >= 2:
            last_phase(t - 2)
        for piece in pieces.get(t, ()):
            piece()
    arrived(UP_X)
    for i in range(3):
        block_load(quarter(i))
        block_compute()
    arrived(UP_LAST)
    block_load(2048 + 3 * FF_BLOCK)
    block_compute()
    block_compute()
    block_ref[...] = yb_ref[...].astype(jnp.bfloat16)
    dgain_ref[...] = jnp.zeros_like(dgain_ref)
    feedforward_back(dy_ref, x2_ref, da2_ref, gain2_ref, dat_ref, dgain_ref)
    attention_backward(
        x_ref, gain1_ref, cos_ref, sin_ref, seg_ref, segt_ref, wq, wk, wv, wo, q_ref, k_ref, v_ref, dat_ref, da2_ref, do_ref, turn_ref, dqf_ref, dkv_ref, dx_ref, dgain_ref
    )
    assert not s_sent and len(done) == FF_BLOCKS
    send.drain()


def layer_pass(parts, tokens, cotangent, seg, position, mine):
    low, full = jnp.bfloat16, jnp.float32
    half = HEAD_WIDTH // 2
    freq = jnp.exp(jnp.arange(half, dtype=full) * (-2.0 * math.log(rope_base) / HEAD_WIDTH))
    angle = position.astype(full)[:, None] * freq[None, :]
    cos, sin = jnp.cos(angle), jnp.sin(angle)
    cos = jnp.tile(cos, (1, 8))
    sin = jnp.tile(jnp.concatenate([-sin, sin], axis=1), (1, 4))
    count = len(GATHER_UNITS)
    outs = [jax.ShapeDtypeStruct((2, 4, 2, *parts[a].shape), low) for a in (4, 5, 6)]
    wide = [(D, low), (D, low), (D, low), (QW, low), (D, low), (FF, low), (QW, low), (2 * KVW, low), (D, low), (FF, low), (FF, low)]
    outs += [jax.ShapeDtypeStruct((ROWS, n), t) for n, t in wide] + [jax.ShapeDtypeStruct((8, D), full)]
    outs += [jax.ShapeDtypeStruct((ROWS, D), low)]
    vmem = pl.BlockSpec(memory_space=pltpu.VMEM)
    scratch = [pltpu.VMEM((2, 4, 2, *parts[a].shape), low) for a in (0, 1, 2, 3, 7)]
    scratch += [pltpu.VMEM((ROWS, D), low), pltpu.VMEM((1, D), full), pltpu.VMEM((1, D), full)]
    scratch += [pltpu.VMEM((2, 2, 4, 2, 96, FF_BLOCK), low)] * 2 + [pltpu.VMEM((2, 2, 256, D), low)]
    scratch += [pltpu.VMEM((n, ROWS, 128), low) for n in (QUERY_HEADS, KEY_VALUE_HEADS, KEY_VALUE_HEADS, QUERY_HEADS)]
    scratch += [pltpu.VMEM((ROWS, D), full), pltpu.VMEM((ROWS, D), full), pltpu.VMEM((ROWS, QW + KVW), full)]
    scratch += [DMA((count, 3))] * 2 + [DMA((count, 2))] * 2 + [DMA((count, 4))] * 2 + [DMA((count, 3))] * 2
    scratch += [DMA((2, MB))] * 2 + [DMA((count, 2)), DMA((2, MB)), DMA((2, 3))]
    scratch += [pltpu.VMEM((parts[a].shape[0], n), low) for a, _, n, _ in GATHER_UNITS]
    results = pl.pallas_call(
        layer_kernel,
        out_shape=outs,
        in_specs=[ANY] * 10 + [vmem] * 5,
        out_specs=[ANY] * 3 + [vmem] * 13,
        scratch_shapes=scratch,
        compiler_params=pltpu.CompilerParams(collective_id=1, has_side_effects=True, vmem_limit_bytes=60 * 2**20),
        name="layer",
    )(*parts, tokens, cotangent, cos, sin, seg.reshape(ROWS, 1), seg.reshape(1, ROWS), mine.astype(jnp.int32).reshape(ROWS, 1))
    return results[3:]


def body(
    tokens,
    query_weight,
    key_weight,
    value_weight,
    out_weight,
    gate_weight,
    up_weight,
    down_weight,
    attention_gain,
    feedforward_gain,
    lengths,
    deal,
    block_cotangent,
):
    me = lax.axis_index("shard")
    core = me % 2
    gains = jnp.pad(jnp.stack([attention_gain, feedforward_gain]), ((0, 0), (0, 32))).reshape(1, 256)
    gains = jnp.pad(gains, ((0, 15), (0, 0)))
    parts = (
        query_weight,
        key_weight,
        value_weight,
        out_weight,
        gate_weight,
        up_weight,
        down_weight,
        gains,
    )
    layout = [window_layout(lengths[m, 0], me * BIN) for m in range(MB)]
    seg = jnp.concatenate([one[0] + m * 64 for m, one in enumerate(layout)])
    position = jnp.concatenate([one[1] for one in layout])
    mine = jnp.concatenate([one[2] for one in layout])
    position = jnp.where(mine, position, 0)
    block_rows, input_rows, a1, o, a2, hid, dqf, dkv, dat, dg, du, dgain, dy = layer_pass(
        parts, tokens, block_cotangent, seg, position, mine
    )

    gain_rows = jnp.pad(dgain.astype(jnp.bfloat16), ((0, 8), (0, 0)))
    arrays = (a1, o, a2, hid, gain_rows, dqf, dkv, dat, dg, du, dy)
    both = exchange(arrays, (True,) * 5 + (False,) * 6)
    a1, o, a2, hid, gain_both, dqf, dkv, dat, dg, du, dy = both
    pairs = ((a1, dqf), (a1, dkv), (o, dat), (a2, dg), (a2, du), (hid, dy))
    grads = [tn(left, right).astype(jnp.bfloat16) for left, right in pairs]
    grads = [grad.reshape(2, 4, -1, grad.shape[-1]) for grad in grads]
    gain_both = gain_both.astype(jnp.float32).reshape(2, 16, D)
    gain_sum = (gain_both[0, :2] + gain_both[1, :2]).reshape(2, 2, 4, 192).transpose(1, 2, 0, 3)
    gain_sum = jnp.pad(gain_sum, ((0, 0), (0, 0), (0, 62), (0, 64))).astype(jnp.bfloat16)
    totals, gain_totals, from_before = reduce_grads(
        (*grads, gain_sum), block_rows.reshape(MB, WIN, D), input_rows.reshape(MB, WIN, D)
    )

    results = jnp.stack([block_rows, input_rows]).reshape(2, MB, WIN, D)[:, :, :BIN]
    from_before = jnp.pad(from_before, ((0, 0), (0, 0), (0, BIN - HALO), (0, 0)))
    mine_own = jnp.stack([one[2][:BIN] for one in layout])[None, :, :, None]
    inside = jnp.stack([one[3][:BIN] for one in layout])[None, :, :, None]
    rows_out = jnp.where(mine_own, results, jnp.where(inside, from_before, 0))
    g_query, g_kv, g_out, g_gate, g_up, g_down = [total.astype(jnp.float32) for total in totals]
    gain_out = lax.dynamic_slice_in_dim(gain_totals[:2].astype(jnp.float32), core * 96, 96, axis=1)
    return (
        rows_out[0],
        rows_out[1],
        g_query,
        g_kv[:, :KVW],
        g_kv[:, KVW:],
        g_out,
        g_gate,
        g_up,
        g_down,
        gain_out[0],
        gain_out[1],
    )


def solution(mesh):
    placed = (
        P(None, ("rep", "shard"), None),
        *([P("shard", None)] * 7),
        P("shard"),
        P("shard"),
        P(None, "rep", None),
        P(None, "rep", None),
        P(None, ("rep", "shard"), None),
    )
    return jax.shard_map(
        body,
        mesh=mesh,
        in_specs=placed,
        out_specs=(
            P(None, ("rep", "shard"), None),
            P(None, ("rep", "shard"), None),
            *([P("shard", None)] * 7),
            P("shard"),
            P("shard"),
        ),
        check_vma=False,
    )
```

profile of v0, /device:TPU:1, one launch (start us, length us, event | category | flops | bytes accessed | tf_op | source)
XLA Modules:
  0.0 447.4 jit_solution(4885223246825413169)
XLA Ops:
  0.7 0.7 fusion.7
  1.4 0.7 slice_bitcast_fusion.9
  2.3 0.7 fusion.9
  3.6 0.6 pad.22.refs_7_
  4.2 0.8 copy.44.refs_14_
  4.9 0.8 copy.43.refs_12_
  5.7 0.3 fusion.1
  6.0 0.9 copy.42.refs_11_
  7.0 0.9 copy.41.refs_10_
  7.9 195.2 %layer.1 = (bf16[2,4,2,96,4096]{4,3,2,1,0:T(8,128)(2,1)}, bf16[2,4,2,96,4096]{4,3,2,1,0:T(8,128)(2,1)}, bf16[2,4,2,256,1536]{4,3,2,1,0:T(8,128)(2,1)}, bf16[224,...) custom-call(bf16[96,1536]{1,0:T(8,128)(2,1)} %refs_0_.1, ...), custom_call_target="tpu_custom_call" | custom-call | tf_op jit(solution)/shard_map/layer/pallas_call | solution.py:727
  203.1 0.8 convert_element_type.86
  203.9 1.5 copy-done
  205.4 1.5 copy-done.1
  206.9 1.5 copy-done.2
  208.4 1.1 copy-done.3
  209.5 1.1 copy-done.4
  210.6 1.1 copy-done.5
  211.7 1.1 copy-done.6
  212.8 1.1 copy-done.7
  213.9 1.1 copy-done.8
  215.0 1.1 copy-done.9
  216.1 17.5 %exchange_rows.1 = (bf16[2,224,1536]{2,1,0:T(8,128)(2,1)S(1)}, bf16[2,224,1536]{2,1,0:T(8,128)(2,1)S(1)}, bf16[2,224,1536]{2,1,0:T(8,128)(2,1)S(1)}, bf16[2,224,...) custom-call(bf16[224,1536]{1,0:T(8,128)(2,1)S(1)} %copy-done.3, ...), custom_call_target="tpu_custom_call" | custom-call | tf_op jit(solution)/shard_map/exchange_rows/pallas_call | solution.py:152
  233.6 1.8 copy-done.10
  235.4 1.3 copy-done.12
  236.7 1.1 copy-done.14
  237.8 1.1 copy-done.16
  238.8 0.8 copy-done.18
  239.7 0.9 copy-done.20
  240.6 0.9 copy-done.22
  241.4 0.8 copy-done.24
  242.4 0.7 pad.24.refs_6_
  243.2 4.5 %bitcast_convert_fusion.5 = bf16[1536,768]{1,0:T(8,128)(2,1)} fusion(bf16[2,224,1536]{2,1,0:T(8,128)(2,1)} %copy-done.16, bf16[2,224,768]{2,1,0:T(8,128)(2,1)} %copy-done.24), kind=kOutput, calls=%fused_computation.5 | convolution fusion | flops 1058144256 | bytes 4423680 | tf_op jit(solution)/shard_map/dot_general | solution.py:361
  247.7 2.9 bitcast_convert_fusion.4
  250.5 2.9 bitcast_convert_fusion.3
  253.5 5.4 %bitcast_convert_fusion.2 = bf16[1536,2048]{1,0:T(8,128)(2,1)} fusion(bf16[2,224,1536]{2,1,0:T(8,128)(2,1)S(1)} %get-tuple-element.61, bf16[2,224,2048]{2,1,0:T(8,128)(2,1)S(1)} %copy-done.13), kind=kOutput, calls=%fused_computation.2 | convolution fusion | flops 2821718016 | bytes 9502720 | tf_op jit(solution)/shard_map/dot_general | solution.py:361
  258.9 5.4 %bitcast_convert_fusion.1 = bf16[1536,2048]{1,0:T(8,128)(2,1)} fusion(bf16[2,224,1536]{2,1,0:T(8,128)(2,1)S(1)} %get-tuple-element.61, bf16[2,224,2048]{2,1,0:T(8,128)(2,1)S(1)} %get-tuple-element.63), kind=kOutput, calls=%fused_computation.1 | convolution fusion | flops 2821718016 | bytes 9502720 | tf_op jit(solution)/shard_map/dot_general | solution.py:361
  264.2 5.6 %bitcast_convert_fusion = bf16[4096,768]{1,0:T(8,128)(2,1)} fusion(bf16[2,224,4096]{2,1,0:T(8,128)(2,1)S(1)} %copy-done.11, bf16[2,224,768]{2,1,0:T(8,128)(2,1)S(1)} %copy-done.19), kind=kOutput, calls=%fused_computation | convolution fusion | flops 2821718016 | bytes 10649600 | tf_op jit(solution)/shard_map/dot_general | solution.py:361
  269.8 167.2 %reduce_grads.1 = (bf16[96,1536]{1,0:T(8,128)(2,1)}, bf16[96,1536]{1,0:T(8,128)(2,1)}, bf16[96,1536]{1,0:T(8,128)(2,1)}, bf16[96,4096]{1,0:T(8,128)(2,1)}, bf16[...) custom-call(bf16[2,4,192,768]{3,2,1,0:T(8,128)(2,1)} %bitcast.82, ...), custom_call_target="tpu_custom_call" | custom-call | tf_op jit(solution)/shard_map/reduce_grads/pallas_call | solution.py:333
  437.0 1.4 fusion
  438.5 0.9 slice_bitcast_fusion
  439.4 0.8 slice.61
  440.2 0.5 slice_bitcast_fusion.6
  440.7 0.9 convert_element_type.94
  441.6 0.9 convert_element_type.96
  442.5 0.9 fusion.12
  443.3 1.3 convert_element_type.97
  444.6 1.3 convert_element_type.98
  445.9 1.3 convert_element_type.99
  (79 shorter events, 1.2 us)
Async XLA Ops:
  3.3 4.5 %copy-start.33 = (s32[224]{0:T(256)}, s32[224]{0:T(256)S(1)}, u32[]{:S(2)}) copy-start(s32[224]{0:T(256)S(1)} %pad_add_fusion.2) | copy-start | bytes 2692
  203.9 1.5 copy-start
  205.4 1.5 copy-start.1
  206.9 1.5 copy-start.2
  208.4 1.1 copy-start.3
  209.5 1.1 copy-start.4
  210.6 1.1 copy-start.5
  211.7 1.1 copy-start.6
  212.8 1.1 copy-start.7
  213.9 1.1 copy-start.8
  215.0 1.1 copy-start.9
  233.6 1.8 copy-start.10
  235.4 1.3 copy-start.12
  236.7 1.1 copy-start.14
  237.8 1.1 copy-start.16
  238.8 0.8 copy-start.18
  239.7 0.9 copy-start.20
  240.5 0.9 copy-start.22
  241.4 0.8 copy-start.24
  243.1 4.5 %copy-start.17 = (bf16[2,224,1536]{2,1,0:T(8,128)(2,1)S(1)}, bf16[2,224,1536]{2,1,0:T(8,128)(2,1)}, u32[]{:S(2)}) copy-start(bf16[2,224,1536]{2,1,0:T(8,128)(2,1)} %copy-done.16) | copy-start | bytes 4128772
  243.2 4.5 %copy-start.23 = (bf16[2,224,768]{2,1,0:T(8,128)(2,1)S(1)}, bf16[2,224,768]{2,1,0:T(8,128)(2,1)}, u32[]{:S(2)}) copy-start(bf16[2,224,768]{2,1,0:T(8,128)(2,1)} %copy-done.22) | copy-start | bytes 2064388
  247.6 2.9 copy-start.15
  247.7 2.9 copy-start.21
  250.5 2.9 copy-start.13
  258.9 5.4 %copy-start.11 = (bf16[2,224,4096]{2,1,0:T(8,128)(2,1)S(1)}, bf16[2,224,4096]{2,1,0:T(8,128)(2,1)}, u32[]{:S(2)}) copy-start(bf16[2,224,4096]{2,1,0:T(8,128)(2,1)} %copy-done.10) | copy-start | bytes 11010052
  258.9 5.4 %copy-start.19 = (bf16[2,224,768]{2,1,0:T(8,128)(2,1)S(1)}, bf16[2,224,768]{2,1,0:T(8,128)(2,1)}, u32[]{:S(2)}) copy-start(bf16[2,224,768]{2,1,0:T(8,128)(2,1)} %copy-done.18) | copy-start | bytes 2064388
  269.8 167.2 %copy-start.25 = (bf16[224,1536]{1,0:T(8,128)(2,1)S(1)}, bf16[224,1536]{1,0:T(8,128)(2,1)}, u32[]{:S(2)}) copy-start(bf16[224,1536]{1,0:T(8,128)(2,1)} %get-tuple-element.43) | copy-start | bytes 2064388
  269.8 167.2 %copy-start.26 = (bf16[224,1536]{1,0:T(8,128)(2,1)S(1)}, bf16[224,1536]{1,0:T(8,128)(2,1)}, u32[]{:S(2)}) copy-start(bf16[224,1536]{1,0:T(8,128)(2,1)} %get-tuple-element.44) | copy-start | bytes 2064388
  437.0 3.7 copy-start.32
  438.4 3.2 copy-start.31
  438.5 4.0 copy-start.27
  439.4 3.9 copy-start.30
  442.5 2.1 copy-start.29
  443.3 2.6 copy-start.28
where the time goes:
time: 451 us; the launch traced here: 447 us
  Pallas kernels  380 us (84%)
  local copies, waits for them, and re-layouts  29.5 us (7%)
  matrix products  26.6 us (6%)
  other arithmetic  10.4 us (2%)
    pallas_call x1, Pallas kernels, layer_pass(): pl.pallas_call(layer_kernel, out_shape=outs, in_specs=[ANY] * 10 + [vmem]...  195 us
    pallas_call x1, Pallas kernels, reduce_grads(): pl.pallas_call(reduce_kernel, out_shape=outs, in_specs=[ANY] * 9, out_spe...  167 us
    dot_general x6, matrix products, dot(): lax.dot_general(a, b, (dims, ((), ())), preferred_element_type=jnp.float32)  26.6 us
    unnamed x69, local copies, waits for them, and re-layouts  20.9 us
    pallas_call x1, Pallas kernels, exchange(): pl.pallas_call(lambda *refs: exchange_kernel(whole, *refs), out_shape=out...  17.5 us

commit v1 on v0

--- a/solution.py
+++ b/solution.py
@@ -115,59 +115,14 @@
     return pl.ds(pl.multiple_of(first, 16), count)
 
 
-def exchange_kernel(whole, *refs):
-    count = len(whole)
-    ins, outs = refs[:count], refs[count : 2 * count]
-    send_sem, recv_sem, local_sem = refs[2 * count : 2 * count + 3]
-    staged = refs[2 * count + 3 :]
-    me = Place()
-    local = []
-    for i, (src, dst) in enumerate(zip(ins, outs)):
-        width = dst.shape[-1]
-        own = src if whole[i] else src.at[:, cut(me.c * width, width)]
-        local.append(pltpu.make_async_copy(own, staged[i], local_sem.at[i, 0]))
-        local[i].start()
-    meet([me.sibling()])
-    send = Sender()
-    for i, (src, dst) in enumerate(zip(ins, outs)):
-        width = dst.shape[-1]
-        theirs = src if whole[i] else src.at[:, cut((1 - me.c) * width, width)]
-        send(theirs, dst.at[me.c], send_sem.at[i], recv_sem.at[i], me.sibling())
-    for i, dst in enumerate(outs):
-        local[i].wait()
-        local[i] = pltpu.make_async_copy(staged[i], dst.at[me.c], local_sem.at[i, 1])
-        local[i].start()
-    for i, copy in enumerate(send.pending):
-        local[i].wait()
-        copy.wait_recv()
-    send.drain()
-
-
-def exchange(arrays, whole):
-    count = len(arrays)
-    outs = []
-    for array, full in zip(arrays, whole):
-        rows, width = array.shape
-        outs.append(jax.ShapeDtypeStruct((2, rows, width if full else width // 2), array.dtype))
-    results = pl.pallas_call(
-        lambda *refs: exchange_kernel(whole, *refs),
-        out_shape=outs,
-        in_specs=[ANY] * count,
-        out_specs=[ANY] * count,
-        scratch_shapes=[DMA((count,))] * 2 + [DMA((count, 2))] + [pltpu.VMEM(out.shape[1:], out.dtype) for out in outs],
-        compiler_params=pltpu.CompilerParams(collective_id=2, has_side_effects=True, vmem_limit_bytes=24 * 2**20),
-        name="exchange_rows",
-    )(*arrays)
-    return [both.reshape(-1, both.shape[-1]) for both in results]
-
-
 REDUCE_ROWS = (192, 192, 192, 192, 192, 512, 64)
 REDUCE_COLUMNS = (768, 768, 768, 2048, 2048, 768, 256)
 REDUCE_DIMS = {"A": "zyx", "B": "yxz", "C": "xzy"}
-REDUCE_UNITS = [("A", 3, i * 512, 512) for i in range(4)] + [("A", 0, 0, 768)]
-REDUCE_UNITS += [("B", 4, i * 512, 512) for i in range(4)] + [("B", 1, 0, 768)]
-REDUCE_UNITS += [("C", 5, i * 256, 256) for i in range(3)] + [("C", 2, 0, 768), ("C", 6, 0, 256)]
-ROUNDS = [(t, 5 + t, 10 + t) for t in range(5)]
+REDUCE_UNITS = [("A", 3, i * 512, 512) for i in range(4)] + [("A", 0, i * 256, 256) for i in range(3)]
+REDUCE_UNITS += [("B", 4, i * 512, 512) for i in range(4)] + [("B", 1, i * 256, 256) for i in range(3)]
+REDUCE_UNITS += [("C", 5, i * 256, 256) for i in range(3)] + [("C", 6, 0, 256)] + [("C", 2, i * 256, 256) for i in range(3)]
+ROUNDS = [(t, 7 + t, 14 + t) for t in range(7)]
+HELD = {"A": (2, 192, 512), "B": (4, 192, 256), "C": (2, 4, 128, 256)}
 GAINS = 6
 
 
@@ -190,25 +145,93 @@
             rest = rest // n
         where = (*where, rcut((i % blocks) * 16, 16), slice(None))
         s = total[where].astype(jnp.float32)
-        for k in range(3):
-            s = s + parts[(k, *where)].astype(jnp.float32)
+        for part in parts:
+            s = s + part[where].astype(jnp.float32)
         total[where] = s.astype(jnp.bfloat16)
         return carry
 
     lax.fori_loop(0, math.prod(lead) * blocks, step, 0)
 
 
+def side(ref, which):
+    count = ref.shape[0] // 2
+    return ref.at[pl.ds(which * count, count)]
+
+
+LEFT_OF = (0, 0, 1, 2, 2, 3)
+LEFTS, RIGHTS = 4, 6
+
+
 def reduce_kernel(*refs):
     nu = len(REDUCE_UNITS)
-    ins, rows_in, outs, halo, totals = refs[:7], refs[7:9], refs[9:16], refs[16], refs[17:24]
-    rest = refs[24:]
+    lefts_hbm, rights_hbm, dgain_hbm, rows_in = refs[:4], refs[4:10], refs[10], refs[11:13]
+    outs, halo, ins, totals = refs[13:20], refs[20], refs[21:28], refs[28:35]
+    rest = refs[35:]
     kept = (rest[:nu], rest[nu : 2 * nu], rest[2 * nu : 3 * nu])
     taken = (rest[3 * nu : 4 * nu], rest[4 * nu : 5 * nu], rest[5 * nu : 6 * nu])
-    send_sem, recv_sem, g_send, g_recv, s_send, s_recv, h_send, h_recv, local_sem, final_sem = rest[6 * nu :]
+    rest = rest[6 * nu :]
+    own_rows, their_rows, tiles, held = rest[:11], rest[11:22], rest[22:25], (rest[25:28], rest[28:31])
+    send_sem, recv_sem, g_send, g_recv, s_send, s_recv, h_send, h_recv, local_sem, final_sem, e_send, e_recv, e_local, tile_sem, ring_send, ring_recv, held_sem = rest[31:]
     me = Place()
+    wanted = (7, 2, 3, 6, 8, 9, 0, 1, 4, 5, 10)
+    own_copies, their_copies = {}, {}
+    sources = (*lefts_hbm, *rights_hbm, dgain_hbm)
+
+    def part(i, core):
+        width = own_rows[i].shape[-1]
+        return sources[i].at[:, cut(core * width, width)] if LEFTS <= i < LEFTS + RIGHTS else sources[i]
+
+    for i in wanted:
+        own_copies[i] = pltpu.make_async_copy(part(i, me.c), own_rows[i], e_local.at[i])
+        own_copies[i].start()
     meet(me.peers("z") + me.peers("x") + me.peers("y") + [me.sibling(), me.step(-1), me.step(1)])
     send = Sender()
     sent, own = {}, {}
+    for i in wanted:
+        their_copies[i] = send(part(i, 1 - me.c), their_rows[i], e_send.at[i], e_recv.at[i], me.sibling())
+
+    def here(*which):
+        for i in which:
+            if i in own_copies:
+                own_copies.pop(i).wait()
+                their_copies.pop(i).wait_recv()
+
+    stored = {}
+
+    def slot_of(u):
+        order, a, _, n = REDUCE_UNITS[u]
+        return "ABC".index(order)
+
+    def product(u):
+        order, a, first, n = REDUCE_UNITS[u]
+        slot = slot_of(u)
+        flush(slot)
+        r = REDUCE_ROWS[a]
+        view = tiles[slot].at[:, :, :r, :n]
+        if a == GAINS:
+            here(10)
+            view[...] = jnp.zeros((2, 4, r, n), jnp.bfloat16)
+            both = own_rows[10][...] + their_rows[10][...]
+            both = jnp.concatenate([both, jnp.zeros_like(both)], axis=0)
+            for k in range(8):
+                tiles[slot][k // 4, k % 4, :16, :192] = both[:, 192 * k : 192 * (k + 1)].astype(jnp.bfloat16)
+        else:
+            left, right = LEFT_OF[a], LEFTS + a
+            here(left, right)
+            for k in range(4):
+                rows, columns = slice(2 * r * k, 2 * r * (k + 1)), slice(first, first + n)
+                value = tn(own_rows[left][:, rows], own_rows[right][:, columns])
+                value = value + tn(their_rows[left][:, rows], their_rows[right][:, columns])
+                view[k // 2, 2 * (k % 2) : 2 * (k % 2) + 2] = value.astype(jnp.bfloat16).reshape(2, r, n)
+        copy = pltpu.make_async_copy(view, ins[a].at[:, :, :, cut(first, n)], tile_sem.at[slot])
+        copy.start()
+        stored[slot] = copy, u
+
+    def flush(slot):
+        if slot in stored:
+            copy, u = stored.pop(slot)
+            copy.wait()
+            issue_first(u)
 
     def share(u, stage, x, yh, yl, z):
         order, a, first, n = REDUCE_UNITS[u]
@@ -230,6 +253,52 @@
             return src.at[yh, :, :, columns]
         return src.at[yh, :, columns]
 
+    ring, holding = {}, {}
+
+    def hold(u):
+        order, a, _, n = REDUCE_UNITS[u]
+        ref = held[u % 7 % 2]["ABC".index(order)]
+        shape = reduce_shapes(u)[0]
+        return ref.at[(*[slice(None)] * (len(shape) - 2), pl.ds(0, shape[-2]), pl.ds(0, shape[-1]))]
+
+    def issue_first(u):
+        right, opposite, left = me.along(REDUCE_DIMS[REDUCE_UNITS[u][0]][0])
+        parts = [share(u, 0, *where) for where in (right, opposite, left)]
+        right, left = me.at(*right), me.at(*left)
+        from_left, from_right, passing = [taken[0][u].at[i] for i in range(3)]
+
+        def go(k, src, dst, to):
+            return send(src, dst, ring_send.at[u, k], ring_recv.at[u, k], to)
+
+        ring[u] = [
+            go(0, side(parts[1], 0), side(passing, 0), right),
+            go(1, side(parts[1], 1), side(passing, 1), left),
+            go(2, side(parts[0], 1), side(from_left, 1), right),
+            go(3, side(parts[2], 0), side(from_right, 0), left),
+        ]
+        holding[u] = [
+            pltpu.make_async_copy(side(parts[0], 0), side(hold(u), 0), held_sem.at[u, 0]),
+            pltpu.make_async_copy(side(parts[2], 1), side(hold(u), 1), held_sem.at[u, 1]),
+        ]
+        own[u, 0] = pltpu.make_async_copy(share(u, 0, me.x, me.yh, me.yl, me.z), kept[0][u], local_sem.at[u, 0])
+        for copy in (*holding[u], own[u, 0]):
+            copy.start()
+
+    def relay(u):
+        right, _, left = me.along(REDUCE_DIMS[REDUCE_UNITS[u][0]][0])
+        from_left, from_right, passing = [taken[0][u].at[i] for i in range(3)]
+        for k, dst, to in ((0, from_left, right), (1, from_right, left)):
+            holding[u][k].wait()
+            ring[u][k].wait_recv()
+            add_into(side(passing, k), [side(hold(u), k)])
+            ring[u].append(send(side(passing, k), side(dst, k), ring_send.at[u, 4 + k], ring_recv.at[u, 4 + k], me.at(*to)))
+
+    def finish_first(u):
+        own[u, 0].wait()
+        for copy in ring[u][2:]:
+            copy.wait_recv()
+        add_into(kept[0][u], [taken[0][u].at[0], taken[0][u].at[1]])
+
     def issue(u, stage):
         dim = REDUCE_DIMS[REDUCE_UNITS[u][0]][stage]
         sent[u, stage] = [
@@ -245,7 +314,7 @@
         own[u, stage].wait()
         for copy in sent[u, stage]:
             copy.wait_recv()
-        add_into(kept[stage][u], taken[stage][u])
+        add_into(kept[stage][u], [taken[stage][u].at[i] for i in range(3)])
 
     def result(u, all_x, all_y):
         order, a, first, n = REDUCE_UNITS[u]
@@ -290,27 +359,32 @@
     for i, src in enumerate(rows_in):
         last.append(send(src.at[:, pl.ds(BIN, HALO)], halo.at[i], h_send.at[i], h_recv.at[i], me.step(1)))
     count = len(ROUNDS)
-    for u in ROUNDS[0]:
-        issue(u, 0)
-    for t in range(count + 4):
+
+    def produce(t):
+        for u in ROUNDS[t]:
+            product(u)
+            for slot in sorted(stored):
+                if slot != slot_of(u):
+                    flush(slot)
+        for slot in sorted(stored):
+            flush(slot)
+
+    produce(0)
+    steps = (
+        (0, relay),
+        (1, lambda u: (finish_first(u), issue(u, 1))),
+        (2, lambda u: (finish(u, 1), issue(u, 2))),
+        (3, lambda u: (finish(u, 2), spread_one(u))),
+        (4, spread_two),
+        (5, deliver),
+    )
+    for t in range(count + 5):
         if t + 1 < count:
-            for u in ROUNDS[t + 1]:
-                issue(u, 0)
-        for stage in range(2):
-            if 0 <= t - stage < count:
-                for u in ROUNDS[t - stage]:
-                    finish(u, stage)
-                    issue(u, stage + 1)
-        if 0 <= t - 2 < count:
-            for u in ROUNDS[t - 2]:
-                finish(u, 2)
-                spread_one(u)
-        if 0 <= t - 3 < count:
-            for u in ROUNDS[t - 3]:
-                spread_two(u)
-        if 0 <= t - 4 < count:
-            for u in ROUNDS[t - 4]:
-                deliver(u)
+            produce(t + 1)
+        for late, step in steps:
+            if 0 <= t - late < count:
+                for u in ROUNDS[t - late]:
+                    step(u)
     for u in range(nu):
         own[u, 5].wait()
     for copy in last:
@@ -318,7 +392,7 @@
     send.drain()
 
 
-def reduce_grads(grads, block_rows, input_rows):
+def reduce_grads(lefts, rights, dgain, block_rows, input_rows):
     nu = len(REDUCE_UNITS)
     first, second, third = zip(*[reduce_shapes(u) for u in range(nu)])
     low = jnp.bfloat16
@@ -326,19 +400,25 @@
     outs = [jax.ShapeDtypeStruct((r // 2, 2 * n), low) for r, n in shapes[:GAINS]]
     outs.append(jax.ShapeDtypeStruct(shapes[GAINS], low))
     outs.append(jax.ShapeDtypeStruct((2, MB, HALO, D), low))
+    outs += [jax.ShapeDtypeStruct((2, 4, r, n), low) for r, n in shapes]
     scratch = [pltpu.VMEM(s, low) for s in shapes]
     scratch += [pltpu.VMEM(s, low) for s in (*first, *second, *third)]
     scratch += [pltpu.VMEM((3, *s), low) for s in (*first, *second, *third)]
+    rows = [pltpu.VMEM(left.shape, low) for left in lefts]
+    rows += [pltpu.VMEM((ROWS, right.shape[1] // 2), low) for right in rights] + [pltpu.VMEM((8, D), jnp.float32)]
+    scratch += rows * 2 + [pltpu.VMEM((2, 4, 192, 512), low)] * 2 + [pltpu.VMEM((2, 4, 512, 256), low)]
+    scratch += [pltpu.VMEM(HELD[order], low) for order in "ABC"] * 2
     scratch += [DMA((nu, 3, 3))] * 2 + [DMA((nu, 6))] * 2 + [DMA((nu,))] * 2 + [DMA((2,))] * 2 + [DMA((nu, 4)), DMA((nu,))]
+    scratch += [DMA((11,))] * 3 + [DMA((3,))] + [DMA((nu, 6))] * 2 + [DMA((nu, 2))]
     results = pl.pallas_call(
         reduce_kernel,
         out_shape=outs,
-        in_specs=[ANY] * 9,
+        in_specs=[ANY] * 13,
         out_specs=[ANY] * len(outs),
         scratch_shapes=scratch,
-        compiler_params=pltpu.CompilerParams(collective_id=3, has_side_effects=True, vmem_limit_bytes=56 * 2**20),
+        compiler_params=pltpu.CompilerParams(collective_id=3, has_side_effects=True, vmem_limit_bytes=60 * 2**20),
         name="reduce_grads",
-    )(*grads, block_rows, input_rows)
+    )(*lefts, *rights, dgain, block_rows, input_rows)
     return results[:GAINS], results[GAINS], results[GAINS + 1]
 
 
@@ -492,10 +572,12 @@
 def layer_kernel(*refs):
     parts, (tokens, cotangent, cos_ref, sin_ref, seg_ref, segt_ref, mine_ref) = refs[:8], refs[8:15]
     wg_hbm, wu_hbm, wd_hbm = refs[15:18]
-    block_ref, dx_ref, a1_ref, o_ref, a2_ref, hid_ref, dqf_ref, dkv_ref, dat_ref, dg_ref, du_ref, dgain_ref, dy_ref = refs[18:31]
+    results = refs[18:31]
     wq, wk, wv, wo, gains_ref, x_ref, gain1_ref, gain2_ref, wg, wu, wd, q_ref, k_ref, v_ref, do_ref, x2_ref, da2_ref, turn_ref = refs[31:49]
-    z_send, z_recv, y_send, y_recv, s_send, s_recv, x_send, x_recv, h_send, h_recv, local_sem, row_sem, block_sem = refs[49:62]
-    staged = refs[62:]
+    rows_out = refs[49:62]
+    block_ref, dx_ref, a1_ref, o_ref, a2_ref, hid_ref, dqf_ref, dkv_ref, dat_ref, dg_ref, du_ref, dgain_ref, dy_ref = rows_out
+    z_send, z_recv, y_send, y_recv, s_send, s_recv, x_send, x_recv, h_send, h_recv, local_sem, row_sem, block_sem, result_sem = refs[62:76]
+    staged = refs[76:]
     outs = (wq, wk, wv, wo, wg_hbm, wu_hbm, wd_hbm, gains_ref)
     me = Place()
     units = GATHER_UNITS
@@ -605,9 +687,18 @@
         at = slice(768 * part, 768 * (part + 1))
         x2_ref[:, at] = x_ref[:, at].astype(jnp.float32) + nn(o_ref[...], wo[:, :, :, :, at].reshape(QW, 768))
 
+    stores = []
+
+    def give(*refs_done):
+        for ref in refs_done:
+            i = [k for k, one in enumerate(rows_out) if one is ref][0]
+            stores.append(pltpu.make_async_copy(ref, results[i], result_sem.at[i]))
+            stores[-1].start()
+
     yb_ref = turn_ref.at[:, :D]
 
     def between():
+        give(a1_ref, o_ref, dy_ref)
         second_norm(x2_ref, gain2_ref, a2_ref)
         yb_ref[...] = x2_ref[...]
         da2_ref[...] = jnp.zeros_like(da2_ref)
@@ -693,12 +784,17 @@
     block_compute()
     block_compute()
     block_ref[...] = yb_ref[...].astype(jnp.bfloat16)
+    give(block_ref, a2_ref, hid_ref, dg_ref, du_ref)
     dgain_ref[...] = jnp.zeros_like(dgain_ref)
     feedforward_back(dy_ref, x2_ref, da2_ref, gain2_ref, dat_ref, dgain_ref)
+    give(dat_ref)
     attention_backward(
         x_ref, gain1_ref, cos_ref, sin_ref, seg_ref, segt_ref, wq, wk, wv, wo, q_ref, k_ref, v_ref, dat_ref, da2_ref, do_ref, turn_ref, dqf_ref, dkv_ref, dx_ref, dgain_ref
     )
-    assert not s_sent and len(done) == FF_BLOCKS
+    give(dqf_ref, dkv_ref, dx_ref, dgain_ref)
+    assert not s_sent and len(done) == FF_BLOCKS and len(stores) == len(rows_out)
+    for copy in stores:
+        copy.wait()
     send.drain()
 
 
@@ -721,14 +817,15 @@
     scratch += [pltpu.VMEM((2, 2, 4, 2, 96, FF_BLOCK), low)] * 2 + [pltpu.VMEM((2, 2, 256, D), low)]
     scratch += [pltpu.VMEM((n, ROWS, 128), low) for n in (QUERY_HEADS, KEY_VALUE_HEADS, KEY_VALUE_HEADS, QUERY_HEADS)]
     scratch += [pltpu.VMEM((ROWS, D), full), pltpu.VMEM((ROWS, D), full), pltpu.VMEM((ROWS, QW + KVW), full)]
+    scratch += [pltpu.VMEM(out.shape, out.dtype) for out in outs[3:]]
     scratch += [DMA((count, 3))] * 2 + [DMA((count, 2))] * 2 + [DMA((count, 4))] * 2 + [DMA((count, 3))] * 2
-    scratch += [DMA((2, MB))] * 2 + [DMA((count, 2)), DMA((2, MB)), DMA((2, 3))]
+    scratch += [DMA((2, MB))] * 2 + [DMA((count, 2)), DMA((2, MB)), DMA((2, 3)), DMA((13,))]
     scratch += [pltpu.VMEM((parts[a].shape[0], n), low) for a, _, n, _ in GATHER_UNITS]
     results = pl.pallas_call(
         layer_kernel,
         out_shape=outs,
         in_specs=[ANY] * 10 + [vmem] * 5,
-        out_specs=[ANY] * 3 + [vmem] * 13,
+        out_specs=[ANY] * 16,
         scratch_shapes=scratch,
         compiler_params=pltpu.CompilerParams(collective_id=1, has_side_effects=True, vmem_limit_bytes=60 * 2**20),
         name="layer",
@@ -774,18 +871,12 @@
         parts, tokens, block_cotangent, seg, position, mine
     )
 
-    gain_rows = jnp.pad(dgain.astype(jnp.bfloat16), ((0, 8), (0, 0)))
-    arrays = (a1, o, a2, hid, gain_rows, dqf, dkv, dat, dg, du, dy)
-    both = exchange(arrays, (True,) * 5 + (False,) * 6)
-    a1, o, a2, hid, gain_both, dqf, dkv, dat, dg, du, dy = both
-    pairs = ((a1, dqf), (a1, dkv), (o, dat), (a2, dg), (a2, du), (hid, dy))
-    grads = [tn(left, right).astype(jnp.bfloat16) for left, right in pairs]
-    grads = [grad.reshape(2, 4, -1, grad.shape[-1]) for grad in grads]
-    gain_both = gain_both.astype(jnp.float32).reshape(2, 16, D)
-    gain_sum = (gain_both[0, :2] + gain_both[1, :2]).reshape(2, 2, 4, 192).transpose(1, 2, 0, 3)
-    gain_sum = jnp.pad(gain_sum, ((0, 0), (0, 0), (0, 62), (0, 64))).astype(jnp.bfloat16)
     totals, gain_totals, from_before = reduce_grads(
-        (*grads, gain_sum), block_rows.reshape(MB, WIN, D), input_rows.reshape(MB, WIN, D)
+        (a1, o, a2, hid),
+        (dqf, dkv, dat, dg, du, dy),
+        dgain,
+        block_rows.reshape(MB, WIN, D),
+        input_rows.reshape(MB, WIN, D),
     )
 
     results = jnp.stack([block_rows, input_rows]).reshape(2, MB, WIN, D)[:, :, :BIN]

time: 451 us -> 379 us (0.84)
  matrix products: 26.6 us -> 0 us
  Pallas kernels: 380 us -> 358 us
  local copies, waits for them, and re-layouts: 29.5 us -> 7.7 us
    dot_general x6 -> x0, matrix products: 26.6 us -> none  [dot(): lax.dot_general(a, b, (dims, ((), ())), preferred_element_type=jnp.float32)]
    unnamed x69 -> x19, local copies, waits for them, and re-layouts: 20.9 us -> 0.04 us
    pallas_call x2 -> x1, Pallas kernels: 185 us -> 166 us  [reduce_grads(): pl.pallas_call(reduce_kernel, out_shape=outs, in_specs=[ANY] * 13, out_sp...]
where the time goes in v1:
time: 379 us; the launch traced here: 376 us
  Pallas kernels  358 us (94%)
  other arithmetic  9.56 us (3%)
  local copies, waits for them, and re-layouts  7.7 us (2%)
    pallas_call x1, Pallas kernels, layer_pass(): pl.pallas_call(layer_kernel, out_shape=outs, in_specs=[ANY] * 10 + [vmem]...  192 us
    pallas_call x1, Pallas kernels, reduce_grads(): pl.pallas_call(reduce_kernel, out_shape=outs, in_specs=[ANY] * 13, out_sp...  166 us

profile of v1, /device:TPU:1, one launch (start us, length us, event | category | flops | bytes accessed | tf_op | source)
XLA Modules:
  0.0 375.9 jit_solution(17479917316376193324)
XLA Ops:
  0.7 0.7 fusion.6
  1.4 0.7 slice_bitcast_fusion.9
  2.1 0.1 select_reduce_fusion.3
  2.2 0.1 select_reduce_fusion.1
  2.3 0.7 fusion.8
  3.0 0.1 convert_reduce_fusion.1
  3.1 0.1 select_reduce_fusion.2
  3.1 0.1 select_reduce_fusion
  3.2 0.1 pad_add_fusion.2
  3.3 0.0 copy-start.8
  3.3 0.1 fusion.2
  3.5 0.1 add_convert_fusion
  3.6 0.6 pad.13.refs_7_
  4.2 0.8 copy.41.refs_14_
  4.9 0.8 copy.40.refs_12_
  5.7 0.3 fusion.1
  6.0 0.9 copy.39.refs_11_
  7.0 0.9 copy.38.refs_10_
  7.9 0.0 copy-done.8
  7.9 191.7 %layer.1 = (bf16[2,4,2,96,4096]{4,3,2,1,0:T(8,128)(2,1)}, bf16[2,4,2,96,4096]{4,3,2,1,0:T(8,128)(2,1)}, bf16[2,4,2,256,1536]{4,3,2,1,0:T(8,128)(2,1)}, bf16[224,...) custom-call(bf16[96,1536]{1,0:T(8,128)(2,1)} %refs_0_.1, ...), custom_call_target="tpu_custom_call" | custom-call | tf_op jit(solution)/shard_map/layer/pallas_call | solution.py:824
  199.5 0.0 copy-start
  199.5 0.0 copy-start.1
  199.6 165.9 %reduce_grads.1 = (bf16[96,1536]{1,0:T(8,128)(2,1)}, bf16[96,1536]{1,0:T(8,128)(2,1)}, bf16[96,1536]{1,0:T(8,128)(2,1)}, bf16[96,4096]{1,0:T(8,128)(2,1)}, bf16[...) custom-call(bf16[224,1536]{1,0:T(8,128)(2,1)} %get-tuple-element.34., ...), custom_call_target="tpu_custom_call" | custom-call | tf_op jit(solution)/shard_map/reduce_grads/pallas_call | solution.py:413
  365.5 0.0 copy-start.7
  365.5 0.0 copy-done
  365.5 0.0 copy-done.1
  365.5 0.0 copy-start.6
  365.5 1.4 fusion
  367.0 0.0 copy-start.2
  367.0 0.0 copy-start.5
  367.0 0.9 slice_bitcast_fusion
  367.9 0.7 slice.53
  368.6 0.1 dynamic-slice_convert_fusion
  368.7 0.5 slice_bitcast_fusion.6
  369.2 0.0 copy-done.7
  369.2 0.9 convert_element_type.56
  370.1 0.0 copy-done.6
  370.1 0.0 copy-start.4
  370.1 0.9 convert_element_type.58
  370.9 0.0 copy-done.2
  370.9 0.9 fusion.11
  371.8 0.0 copy-done.5
  371.8 0.0 copy-start.3
  371.8 1.3 convert_element_type.59
  373.1 0.0 copy-done.4
  373.1 1.3 convert_element_type.60
  374.4 0.0 copy-done.3
  374.4 1.3 convert_element_type.61
  (15 shorter events, 0.1 us)
Async XLA Ops:
  3.3 4.5 %copy-start.8 = (s32[224]{0:T(256)}, s32[224]{0:T(256)S(1)}, u32[]{:S(2)}) copy-start(s32[224]{0:T(256)S(1)} %pad_add_fusion.2) | copy-start | bytes 2692
  199.5 166.0 %copy-start = (bf16[224,1536]{1,0:T(8,128)(2,1)S(1)}, bf16[224,1536]{1,0:T(8,128)(2,1)}, u32[]{:S(2)}) copy-start(bf16[224,1536]{1,0:T(8,128)(2,1)} %get-tuple-element.32) | copy-start | bytes 2064388
  199.5 166.0 %copy-start.1 = (bf16[224,1536]{1,0:T(8,128)(2,1)S(1)}, bf16[224,1536]{1,0:T(8,128)(2,1)}, u32[]{:S(2)}) copy-start(bf16[224,1536]{1,0:T(8,128)(2,1)} %get-tuple-element.33) | copy-start | bytes 2064388
  365.5 3.7 copy-start.7
  365.5 4.6 %copy-start.6 = (bf16[96,1536]{1,0:T(8,128)(2,1)S(1)}, bf16[96,1536]{1,0:T(8,128)(2,1)}, u32[]{:S(2)}) copy-start(bf16[96,1536]{1,0:T(8,128)(2,1)} %get-tuple-element.48) | copy-start | bytes 884740
  367.0 4.0 %copy-start.2 = (bf16[96,1536]{1,0:T(8,128)(2,1)S(1)}, bf16[96,1536]{1,0:T(8,128)(2,1)}, u32[]{:S(2)}) copy-start(bf16[96,1536]{1,0:T(8,128)(2,1)} %get-tuple-element.47) | copy-start | bytes 884740
  367.0 4.8 %copy-start.5 = (bf16[96,4096]{1,0:T(8,128)(2,1)S(1)}, bf16[96,4096]{1,0:T(8,128)(2,1)}, u32[]{:S(2)}) copy-start(bf16[96,4096]{1,0:T(8,128)(2,1)} %get-tuple-element.49) | copy-start | bytes 2359300
  370.1 3.0 copy-start.4
  371.8 2.6 copy-start.3
